TPU v7x, 32 devices: a whole 2x2x4 slice. The times are simulated.
32 devices in a mesh: groups: 2 (over x), sensor: 8 (over z, y), seg: 2 (over core).
Axes of the slice: x: 2, y: 2, z: 4, core: 2. Of those that a mesh axis runs over, the one named last changes fastest.
Arguments:
- traces: bfloat16 [2, 512, 4096], P('seg', ('groups', 'sensor')), parts along dimension 1, may hold values from -40 to 40
- fir_taps: bfloat16 [512, 255], P(('groups', 'sensor')), parts along dimension 0, may hold values from -0.375 to 0.375
- slot_channel: int32 [16, 32], P(('groups', 'sensor')), parts along dimension 0, may hold values from 0 to 31, each once within a row
- segment_valid: int32 [2, 512], P('seg', ('groups', 'sensor')), parts along dimension 1, may hold values 0 or 1
- distances: int32 [2], replicated, may hold values from 1 to 7, as said below
Outputs:
- pair_sums: float32 [2, 512, 1536], P(None, ('groups', 'sensor'), 'seg'), parts along dimension 1
There are 2 independent parts, one for each index of `groups`. A program takes and returns all parts, laid end to end along the dimension named above; an argument that names none is the same for every part. Nothing has to cross between parts.
Inputs may be any that keep to these rules, and one draw needn't show every extreme that they name: `slot_channel`: each row lists every slot index of a block once. `distances`: one entry, at a position drawn anew, is 7.
All inputs are finite; a program needn't handle non-finite values. No bound on the sum of `segment_valid` on one device may be relied on, other than what follows from the above.
Results may differ from a plain program's by a relative error of at most 0.004.
Values may be sent and summed in bfloat16 or wider, within the bound.
A program may use at most 64 MiB of HBM per device.

v0:
```python
import functools
import math

import jax
import jax.numpy as jnp
from jax import lax
from jax.experimental import pallas as pl
from jax.experimental.pallas import tpu as pltpu
from jax.sharding import PartitionSpec as P

LAGS = 48
FINE = 8
COARSE = LAGS // FINE
LANES = 128
EPSILON = 1e-06
NT = (((1,), (1,)), ((), ()))


def whiten_kernel(slot_ref, valid_ref, traces_ref, taps_ref, out_ref, rows_ref, taps_f32):
    channels, samples = traces_ref.shape[1:]
    tap_count = taps_ref.shape[1]
    pieces = samples // LANES
    margin = (tap_count - 1) // 2
    width = 3 * LANES
    rows_ref[0:channels] = jnp.zeros((channels, LANES), jnp.float32)
    rows_ref[(pieces + 1) * channels :] = jnp.zeros((channels, LANES), jnp.float32)
    for piece in range(pieces):
        rows_ref[(piece + 1) * channels : (piece + 2) * channels] = traces_ref[
            0, :, piece * LANES : (piece + 1) * LANES
        ].astype(jnp.float32)
    taps_f32[...] = jnp.zeros_like(taps_f32)
    taps_f32[:, 0:tap_count] = taps_ref[...].astype(jnp.float32)

    @pl.loop(0, channels, unroll=4)
    def _(slot):
        channel = slot_ref[0, slot]
        usable = valid_ref[0, channel].astype(jnp.float32)
        windows = jnp.concatenate(
            [
                rows_ref[pl.ds(piece * channels + channel, pieces, stride=channels)].astype(jnp.bfloat16)
                for piece in range(3)
            ],
            axis=1,
        )
        filter_row = jnp.broadcast_to(taps_f32[pl.ds(channel, 1)], (LANES, width))
        banded = pltpu.roll(filter_row, LANES - margin, 1, stride=1, stride_axis=0)
        filtered = lax.dot_general(
            windows, banded.astype(jnp.bfloat16), NT, preferred_element_type=jnp.float32
        )
        energy = jnp.sum(filtered * filtered, keepdims=True) * (1.0 / samples)
        scaled = filtered * (lax.rsqrt(energy + EPSILON) * usable)
        out_ref[pl.ds(slot, pieces, stride=channels)] = scaled


def shifted(now, following, amount):
    if amount == 0:
        return now
    lane = lax.broadcasted_iota(jnp.int32, now.shape, 1)
    rolled = [pltpu.roll(x, LANES - amount, 1) for x in (now, following)]
    return jnp.where(lane < LANES - amount, rolled[0], rolled[1])


def correlate_kernel(own_ref, first_ref, second_ref, out_ref, left_ref, right_ref):
    pieces, channels, _ = own_ref.shape
    half = channels // 2
    before = LAGS // 2
    zero = jnp.zeros((channels, LANES), jnp.float32)

    def piece_of(ref, piece):
        if piece < 0 or piece >= pieces:
            return zero
        return ref[piece].astype(jnp.float32)

    for piece in range(-1, pieces):
        lanes = slice((piece + 1) * LANES, (piece + 2) * LANES)
        for coarse in range(COARSE):
            amount = before - FINE * coarse
            if amount >= 0:
                value = shifted(piece_of(own_ref, piece), piece_of(own_ref, piece + 1), amount)
            else:
                value = shifted(piece_of(own_ref, piece - 1), piece_of(own_ref, piece), LANES + amount)
            left_ref[coarse * channels : (coarse + 1) * channels, lanes] = value.astype(jnp.bfloat16)
        for round_index, ref in enumerate((first_ref, second_ref)):
            for fine in range(FINE):
                value = shifted(piece_of(ref, piece), piece_of(ref, piece + 1), fine).astype(jnp.bfloat16)
                for part in range(2):
                    row = part * 2 * FINE * half + round_index * FINE * half + fine * half
                    right_ref[row : row + half, lanes] = value[part * half : (part + 1) * half]
    products = lax.dot_general(left_ref[...], right_ref[...], NT, preferred_element_type=jnp.float32)
    columns = products.shape[1] // 2
    out_ref[0] = products[:, :columns]
    out_ref[1] = products[:, columns:]


def arrange_kernel(factor, sums_ref, out_ref, table_ref):
    round_count, channels, columns = out_ref.shape
    half = channels // 2
    width = FINE * half
    for coarse in range(COARSE):
        row = lax.broadcasted_iota(jnp.int32, (width, columns), 0)
        column = lax.broadcasted_iota(jnp.int32, (width, columns), 1)
        target = (row % half) * LAGS + row // half + coarse * FINE
        table_ref[coarse * width : (coarse + 1) * width] = jnp.where(column == target, 1.0, 0.0).astype(jnp.bfloat16)
    gathered = jnp.concatenate(
        [
            jnp.concatenate(
                [
                    sums_ref[coarse * channels : (coarse + 1) * channels, r * width : (r + 1) * width]
                    for coarse in range(COARSE)
                ],
                axis=1,
            )
            for r in range(round_count)
        ],
        axis=0,
    ) * factor
    top = gathered.astype(jnp.bfloat16)
    rest = gathered - top.astype(jnp.float32)
    middle = rest.astype(jnp.bfloat16)
    low = (rest - middle.astype(jnp.float32)).astype(jnp.bfloat16)
    stacked = jnp.concatenate([top, middle, low], axis=0)
    moved = jnp.dot(stacked, table_ref[...], preferred_element_type=jnp.float32)
    count = round_count * channels
    result = moved[:count] + (moved[count : 2 * count] + moved[2 * count :])
    for r in range(round_count):
        out_ref[r] = result[r * channels : (r + 1) * channels]


def swapped(value, mask):
    pairs = [(source, source ^ mask) for source in range(lax.axis_size("sensor"))]
    return lax.ppermute(value, "sensor", pairs)


def shards(traces, fir_taps, slot_channel, segment_valid, distances):
    _, channels, samples = traces.shape
    pieces = samples // LANES
    half = channels // 2
    vmem = pl.BlockSpec(memory_space=pltpu.VMEM)
    smem = pl.BlockSpec(memory_space=pltpu.SMEM)
    params = pltpu.CompilerParams(vmem_limit_bytes=48 * 2**20)
    whitened = pl.pallas_call(
        whiten_kernel,
        out_shape=jax.ShapeDtypeStruct((pieces * channels, LANES), jnp.float32),
        in_specs=[smem, smem, vmem, vmem],
        out_specs=vmem,
        scratch_shapes=[
            pltpu.VMEM(((pieces + 2) * channels, LANES), jnp.float32),
            pltpu.VMEM((channels, 3 * LANES), jnp.float32),
        ],
        compiler_params=params,
    )(slot_channel, segment_valid, traces, fir_taps)
    whitened = whitened.astype(jnp.bfloat16).reshape(pieces, channels, LANES)

    blocks = lax.axis_size("sensor")
    farthest = blocks - 1
    opposite = swapped(whitened, farthest)
    first_far = distances[0] == farthest
    other = jnp.where(first_far, distances[1], distances[0])
    crosses = other >= blocks // 2
    carried = jnp.where(crosses, opposite, whitened)
    rest = jnp.where(crosses, jnp.bitwise_xor(other, farthest), other)
    for bit in range(farthest.bit_length() - 1):
        chosen = jnp.bitwise_and(jnp.right_shift(rest, bit), 1) == 1
        carried = jnp.where(chosen, swapped(carried, 1 << bit), carried)
    first = jnp.where(first_far, opposite, carried)
    second = jnp.where(first_far, carried, opposite)

    depth = (pieces + 1) * LANES
    products = pl.pallas_call(
        correlate_kernel,
        out_shape=jax.ShapeDtypeStruct((2, COARSE * channels, 2 * FINE * half), jnp.float32),
        in_specs=[vmem] * 3,
        out_specs=vmem,
        scratch_shapes=[
            pltpu.VMEM((COARSE * channels, depth), jnp.bfloat16),
            pltpu.VMEM((2 * FINE * channels, depth), jnp.bfloat16),
        ],
        compiler_params=params,
    )(whitened, first, second)
    summed = lax.psum_scatter(products, "seg", scatter_dimension=0, tiled=False)
    factor = 1.0 / math.sqrt(samples * traces.shape[0] * lax.axis_size("seg"))
    return pl.pallas_call(
        functools.partial(arrange_kernel, factor),
        out_shape=jax.ShapeDtypeStruct((2, channels, half * LAGS), jnp.float32),
        in_specs=[vmem],
        out_specs=vmem,
        scratch_shapes=[pltpu.VMEM((COARSE * FINE * half, half * LAGS), jnp.bfloat16)],
        compiler_params=params,
    )(summed)


def solution(mesh):
    placed = (
        P("seg", ("groups", "sensor"), None),
        P(("groups", "sensor"), None),
        P(("groups", "sensor"), None),
        P("seg", ("groups", "sensor")),
        P(),
    )
    return jax.shard_map(
        shards,
        mesh=mesh,
        in_specs=placed,
        out_specs=P(None, ("groups", "sensor"), "seg"),
        check_vma=False,
    )
```

profile of v0, /device:TPU:1, one launch (start us, length us, event | category | flops | bytes accessed | tf_op | source)
XLA Modules:
  0.0 65.5 jit_solution(2814274253706865442)
XLA Ops:
  6.5 0.0 reduce-scatter.2.cloned.1.call-start
  6.5 0.0 copy-start
  6.5 0.9 %copy-done = bf16[1,32,4096]{2,1,0:T(8,128)(2,1)S(1)} copy-done((bf16[1,32,4096]{2,1,0:T(8,128)(2,1)S(1)}, bf16[1,32,4096]{2,1,0:T(8,128)(2,1)}, u32[]{:S(2)}) %copy-start) | copy-done | bytes 262168
  7.5 0.0 copy-start.2
  7.5 0.7 %copy-done.2 = bf16[32,255]{1,0:T(8,128)(2,1)S(1)} copy-done((bf16[32,255]{1,0:T(8,128)(2,1)S(1)}, bf16[32,255]{1,0:T(8,128)(2,1)}, u32[]{:S(2)}) %copy-start.2) | copy-done | bytes 16344
  8.2 0.0 copy-start.3
  8.2 0.7 copy-done.3
  8.9 0.0 copy-start.4
  8.9 0.7 copy-done.4
  9.5 4.9 %shard_map.55 = f32[1024,128]{1,0:T(8,128)S(1)} custom-call(s32[1,32]{1,0:T(1,128)S(1)} %copy-done.3, s32[1,32]{1,0:T(1,128)S(1)} %copy-done.4, bf16[1,32,4096]{2,1,0:T(8,128)(2,1)S(1)} %copy-done, bf16[32,255]{1,0:T(8,128)(2,1)S(1)} %copy-done.2), custom_call_target="tpu_custom_call" | custom-call | tf_op jit(solution)/shard_map/pallas_call | solution.py:141
  14.4 0.0 copy-start.5
  14.5 5.2 %collective-permute-start = (bf16[32,32,128]{2,1,0:T(8,128)(2,1)S(1)}, bf16[32,32,128]{2,1,0:T(8,128)(2,1)S(1)}, u32[]{:S(2)}, u32[]{:S(2)}) collective-permute-start(bf16[32,32,128]{2,1,0:T(8,128)(2,1)S(1)} %bitcast.4), channel_id=1, source_target_pairs={{0,14},{2,12},{4,10},{6,8},{8,6},{10,4},{12,2},{14,0},{1,15},{3,13... | collective-permute-start | bytes 786440 | tf_op jit(solution)/shard_map/ppermute | solution.py:131
  19.6 0.0 copy-done.5
  19.6 0.6 fusion
  22.1 3.6 %collective-permute-done = bf16[32,32,128]{2,1,0:T(8,128)(2,1)S(1)} collective-permute-done((bf16[32,32,128]{2,1,0:T(8,128)(2,1)S(1)}, bf16[32,32,128]{2,1,0:T(8,128)(2,1)S(1)}, u32[]{:S(2)}, u32[]{:S(2)}) %collective-permute-start) | collective-permute-done | bytes 262176 | tf_op jit(solution)/shard_map/ppermute | solution.py:131
  25.7 0.9 %collective-permute-start.1 = (bf16[32,32,128]{2,1,0:T(8,128)(2,1)S(1)}, bf16[32,32,128]{2,1,0:T(8,128)(2,1)S(1)}, u32[]{:S(2)}, u32[]{:S(2)}) collective-permute-start(bf16[32,32,128]{2,1,0:T(8,128)(2,1)S(1)} %broadcast_select_fusion), channel_id=1, source_target_pairs={{0,2},{2,0},{4,6},{6,4},{8,10},{10,8},{12,14},{14,12},{1,3},{3,1},... | collective-permute-start | bytes 786440 | tf_op jit(solution)/shard_map/ppermute | solution.py:131
  26.7 5.7 %collective-permute-done.1 = bf16[32,32,128]{2,1,0:T(8,128)(2,1)S(1)} collective-permute-done((bf16[32,32,128]{2,1,0:T(8,128)(2,1)S(1)}, bf16[32,32,128]{2,1,0:T(8,128)(2,1)S(1)}, u32[]{:S(2)}, u32[]{:S(2)}) %collective-permute-start.1) | collective-permute-done | bytes 262176 | tf_op jit(solution)/shard_map/ppermute | solution.py:131
  32.4 4.7 %collective-permute-start.2 = (bf16[32,32,128]{2,1,0:T(8,128)(2,1)S(1)}, bf16[32,32,128]{2,1,0:T(8,128)(2,1)S(1)}, u32[]{:S(2)}, u32[]{:S(2)}) collective-permute-start(bf16[32,32,128]{2,1,0:T(8,128)(2,1)S(1)} %broadcast_select_fusion.1), channel_id=1, source_target_pairs={{0,4},{2,6},{4,0},{6,2},{8,12},{10,14},{12,8},{14,10},{1,5},{3,7},... | collective-permute-start | bytes 786440 | tf_op jit(solution)/shard_map/ppermute | solution.py:131
  37.0 4.3 %collective-permute-done.2 = bf16[32,32,128]{2,1,0:T(8,128)(2,1)S(1)} collective-permute-done((bf16[32,32,128]{2,1,0:T(8,128)(2,1)S(1)}, bf16[32,32,128]{2,1,0:T(8,128)(2,1)S(1)}, u32[]{:S(2)}, u32[]{:S(2)}) %collective-permute-start.2) | collective-permute-done | bytes 262176 | tf_op jit(solution)/shard_map/ppermute | solution.py:131
  41.4 4.3 %shard_map.56 = f32[2,192,256]{2,1,0:T(8,128)} custom-call(bf16[32,32,128]{2,1,0:T(8,128)(2,1)S(1)} %bitcast.6, bf16[32,32,128]{2,1,0:T(8,128)(2,1)S(1)} %get-tuple-element.6.first_ref, bf16[32,32,128]{2,1,0:T(8,128)(2,1)S(1)} %get-tuple-element.5.second_ref), custom_call_target="tpu_custom_call" | custom-call | tf_op jit(solution)/shard_map/pallas_call | solution.py:169
  45.7 0.0 reduce-scatter.2.cloned.1.call-update
  45.7 10.9 %reduce-scatter.2.cloned.1.call-done = f32[1,192,256]{2,1,0:T(8,128)} async-done(((f32[2,192,256]{2,1,0:T(8,128)}), f32[1,192,256]{2,1,0:T(8,128)}) %reduce-scatter.2.cloned.1.call-update) | async-done | bytes 196624 | tf_op jit(solution)/shard_map/reduce_scatter | solution.py:180
  56.6 0.9 %copy-done.1 = f32[1,192,256]{2,1,0:T(8,128)S(1)} copy-done((f32[1,192,256]{2,1,0:T(8,128)S(1)}, f32[1,192,256]{2,1,0:T(8,128)}, u32[]{:S(2)}) %copy-start.1) | copy-done | bytes 196632
  57.5 1.1 %shard_map.57 = f32[2,32,768]{2,1,0:T(8,128)} custom-call(f32[192,256]{1,0:T(8,128)S(1)} %bitcast.7), custom_call_target="tpu_custom_call" | custom-call | tf_op jit(solution)/shard_map/pallas_call | solution.py:182
  (5 shorter events, 0.1 us)
Async XLA Ops:
  6.5 50.0 %reduce-scatter.2.cloned.1.call-start = ((), (), s32[]{:S(2)}) async-start(), calls=%async_computation.1 | async-start | bytes 589824 | tf_op jit(solution)/shard_map/reduce_scatter | solution.py:180
  6.5 0.9 %copy-start = (bf16[1,32,4096]{2,1,0:T(8,128)(2,1)S(1)}, bf16[1,32,4096]{2,1,0:T(8,128)(2,1)}, u32[]{:S(2)}) copy-start(bf16[1,32,4096]{2,1,0:T(8,128)(2,1)} %traces_ref.1) | copy-start | bytes 786436
  7.5 0.7 %copy-start.2 = (bf16[32,255]{1,0:T(8,128)(2,1)S(1)}, bf16[32,255]{1,0:T(8,128)(2,1)}, u32[]{:S(2)}) copy-start(bf16[32,255]{1,0:T(8,128)(2,1)} %taps_ref.1) | copy-start | bytes 48964
  8.2 0.7 %copy-start.3 = (s32[1,32]{1,0:T(1,128)S(1)}, s32[1,32]{1,0:T(1,128)}, u32[]{:S(2)}) copy-start(s32[1,32]{1,0:T(1,128)} %slot_ref.1) | copy-start | bytes 388
  8.9 0.7 %copy-start.4 = (s32[1,32]{1,0:T(1,128)S(1)}, s32[1,32]{1,0:T(1,128)}, u32[]{:S(2)}) copy-start(s32[1,32]{1,0:T(1,128)} %valid_ref.1) | copy-start | bytes 388
  14.4 5.2 %copy-start.5 = (s32[2]{0:T(128)S(1)}, s32[2]{0:T(128)}, u32[]{:S(2)}) copy-start(s32[2]{0:T(128)} %param.9) | copy-start | bytes 28
  14.5 11.3 %collective-permute-start = (bf16[32,32,128]{2,1,0:T(8,128)(2,1)S(1)}, bf16[32,32,128]{2,1,0:T(8,128)(2,1)S(1)}, u32[]{:S(2)}, u32[]{:S(2)}) collective-permute-start(bf16[32,32,128]{2,1,0:T(8,128)(2,1)S(1)} %bitcast.4), channel_id=1, source_target_pairs={{0,14},{2,12},{4,10},{6,8},{8,6},{10,4},{12,2},{14,0},{1,15},{3,13... | collective-permute-start | bytes 786440 | tf_op jit(solution)/shard_map/ppermute | solution.py:131
  25.7 6.6 %collective-permute-start.1 = (bf16[32,32,128]{2,1,0:T(8,128)(2,1)S(1)}, bf16[32,32,128]{2,1,0:T(8,128)(2,1)S(1)}, u32[]{:S(2)}, u32[]{:S(2)}) collective-permute-start(bf16[32,32,128]{2,1,0:T(8,128)(2,1)S(1)} %broadcast_select_fusion), channel_id=1, source_target_pairs={{0,2},{2,0},{4,6},{6,4},{8,10},{10,8},{12,14},{14,12},{1,3},{3,1},... | collective-permute-start | bytes 786440 | tf_op jit(solution)/shard_map/ppermute | solution.py:131
  32.4 9.0 %collective-permute-start.2 = (bf16[32,32,128]{2,1,0:T(8,128)(2,1)S(1)}, bf16[32,32,128]{2,1,0:T(8,128)(2,1)S(1)}, u32[]{:S(2)}, u32[]{:S(2)}) collective-permute-start(bf16[32,32,128]{2,1,0:T(8,128)(2,1)S(1)} %broadcast_select_fusion.1), channel_id=1, source_target_pairs={{0,4},{2,6},{4,0},{6,2},{8,12},{10,14},{12,8},{14,10},{1,5},{3,7},... | collective-permute-start | bytes 786440 | tf_op jit(solution)/shard_map/ppermute | solution.py:131
  56.6 0.9 %copy-start.1 = (f32[1,192,256]{2,1,0:T(8,128)S(1)}, f32[1,192,256]{2,1,0:T(8,128)}, u32[]{:S(2)}) copy-start(f32[1,192,256]{2,1,0:T(8,128)} %reduce-scatter.2.cloned.1.call-done) | copy-start | bytes 589828
Sparse Core Ops, SparseCore 0:
  45.8 10.7 reduce-scatter.1
where the time goes:
time: 66 us; the launch traced here: 65.5 us
  waiting for transfers between devices  24.4 us (37%)
  between operations  15.3 us (23%)
  starting transfers between devices  10.8 us (16%)
  Pallas kernels  10.3 us (16%)
  local copies, waits for them, and re-layouts  4.49 us (7%)
    ppermute x3, waiting for transfers between devices, swapped(): return lax.ppermute(value, 'sensor', pairs)  13.5 us
    reduce_scatter x1, waiting for transfers between devices, shards(): summed = lax.psum_scatter(products, 'seg', scatter_dimension=0, tiled=False)  10.9 us
    ppermute x3, starting transfers between devices, swapped(): return lax.ppermute(value, 'sensor', pairs)  10.8 us
    pallas_call x1, Pallas kernels, shards(): pl.pallas_call(whiten_kernel, out_shape=jax.ShapeDtypeStruct((pieces * ch...  4.89 us
    pallas_call x1, Pallas kernels, shards(): pl.pallas_call(correlate_kernel, out_shape=jax.ShapeDtypeStruct((2, COARS...  4.29 us
    unnamed x12, local copies, waits for them, and re-layouts  3.91 us
  transfers between devices with their start and end apart: 4, of which 4 were waited for; matrix products, arithmetic and copies ran while one was open for 1% of the time, Pallas kernels for 0%

commit v1 on v0

v1 whole, which is shorter than its diff:
```python
import functools
import math

import jax
import jax.numpy as jnp
from jax import lax
from jax.experimental import pallas as pl
from jax.experimental.pallas import tpu as pltpu
from jax.sharding import PartitionSpec as P

LAGS = 48
FINE = 8
COARSE = LAGS // FINE
LANES = 128
CHUNKS = 4
EPSILON = 1e-06
NT = (((1,), (1,)), ((), ()))


def whiten_kernel(
    slot_hbm, valid_hbm, traces_hbm, taps_hbm, out_ref, slot_ref, valid_ref, traces_ref, taps_ref,
    rows_ref, taps_f32, scaled_ref, sems,
):
    copies = [
        pltpu.make_async_copy(source, target, sems.at[index])
        for index, (source, target) in enumerate(
            [(traces_hbm, traces_ref), (taps_hbm, taps_ref), (slot_hbm, slot_ref), (valid_hbm, valid_ref)]
        )
    ]
    for copy in copies:
        copy.start()
    for copy in copies:
        copy.wait()
    channels, samples = traces_ref.shape[1:]
    tap_count = taps_ref.shape[1]
    pieces = samples // LANES
    margin = (tap_count - 1) // 2
    width = 3 * LANES
    rows_ref[0:channels] = jnp.zeros((channels, LANES), jnp.float32)
    rows_ref[(pieces + 1) * channels :] = jnp.zeros((channels, LANES), jnp.float32)
    for piece in range(pieces):
        rows_ref[(piece + 1) * channels : (piece + 2) * channels] = traces_ref[
            0, :, piece * LANES : (piece + 1) * LANES
        ].astype(jnp.float32)
    taps_f32[...] = jnp.zeros_like(taps_f32)
    taps_f32[:, 0:tap_count] = taps_ref[...].astype(jnp.float32)

    @pl.loop(0, channels, unroll=4)
    def _(slot):
        channel = slot_ref[0, slot]
        usable = valid_ref[0, channel].astype(jnp.float32)
        windows = jnp.concatenate(
            [
                rows_ref[pl.ds(piece * channels + channel, pieces, stride=channels)].astype(jnp.bfloat16)
                for piece in range(3)
            ],
            axis=1,
        )
        filter_row = jnp.broadcast_to(taps_f32[pl.ds(channel, 1)], (LANES, width))
        banded = pltpu.roll(filter_row, LANES - margin, 1, stride=1, stride_axis=0)
        filtered = lax.dot_general(
            windows, banded.astype(jnp.bfloat16), NT, preferred_element_type=jnp.float32
        )
        energy = jnp.sum(filtered * filtered, keepdims=True) * (1.0 / samples)
        scaled = filtered * (lax.rsqrt(energy + EPSILON) * usable)
        scaled_ref[pl.ds(slot, pieces, stride=channels)] = scaled

    for piece in range(pieces):
        out_ref[piece] = scaled_ref[piece * channels : (piece + 1) * channels].astype(jnp.bfloat16)


def shifted(now, following, amount):
    if amount == 0:
        return now
    lane = lax.broadcasted_iota(jnp.int32, now.shape, 1)
    rolled = [pltpu.roll(x, LANES - amount, 1) for x in (now, following)]
    return jnp.where(lane < LANES - amount, rolled[0], rolled[1])


def arrange(table_ref, parts, factor):
    rows = jnp.concatenate(parts, axis=0) * factor
    top = rows.astype(jnp.bfloat16)
    rest = rows - top.astype(jnp.float32)
    middle = rest.astype(jnp.bfloat16)
    low = (rest - middle.astype(jnp.float32)).astype(jnp.bfloat16)
    stacked = jnp.concatenate([top, middle, low], axis=0)
    moved = jnp.dot(stacked, table_ref[...], preferred_element_type=jnp.float32)
    count = rows.shape[0]
    return moved[:count] + (moved[count : 2 * count] + moved[2 * count :])


def exchange_kernel(
    blocks, factor, distances_ref, own_ref, out_ref, padded_ref, far_ref, carried_ref, arrived_ref,
    left_ref, right_ref, products_ref, sums_ref, table_ref, far_sems, hop_sems, sum_sems,
):
    pieces, channels, _ = own_ref.shape
    half = channels // 2
    before = LAGS // 2
    width = FINE * half
    farthest = blocks - 1
    hops = farthest.bit_length() - 1
    per_chunk = pieces // CHUNKS
    me = lax.axis_index("sensor")
    seg = lax.axis_index("seg")

    def partner(mask):
        result = 0
        for bit in range(farthest.bit_length()):
            value = lax.rem(lax.div(me, 1 << bit), 2)
            result = result + ((1 - value) if (mask >> bit) & 1 else value) * (1 << bit)
        return {"sensor": result}

    barrier = pltpu.get_barrier_semaphore()
    others = [partner(farthest)] + [partner(1 << bit) for bit in range(hops)] + [{"seg": 1 - seg}]
    for other in others:
        pl.semaphore_signal(barrier, inc=1, device_id=other, device_id_type=pl.DeviceIdType.MESH)
    pl.semaphore_wait(barrier, len(others))

    def far_copy(chunk):
        return pltpu.make_async_remote_copy(
            src_ref=own_ref.at[pl.ds(chunk * per_chunk, per_chunk)],
            dst_ref=far_ref.at[pl.ds(1 + chunk * per_chunk, per_chunk)],
            send_sem=far_sems.at[0, chunk],
            recv_sem=far_sems.at[1, chunk],
            device_id=others[0],
            device_id_type=pl.DeviceIdType.MESH,
        )

    def hop_copy(bit, chunk):
        return pltpu.make_async_remote_copy(
            src_ref=carried_ref.at[bit, pl.ds(1 + chunk * per_chunk, per_chunk)],
            dst_ref=arrived_ref.at[bit, pl.ds(chunk * per_chunk, per_chunk)],
            send_sem=hop_sems.at[0, bit, chunk],
            recv_sem=hop_sems.at[1, bit, chunk],
            device_id=others[1 + bit],
            device_id_type=pl.DeviceIdType.MESH,
        )

    def sum_copy(which):
        return pltpu.make_async_remote_copy(
            src_ref=products_ref.at[which, 1 - seg],
            dst_ref=sums_ref.at[which],
            send_sem=sum_sems.at[0, which],
            recv_sem=sum_sems.at[1, which],
            device_id=others[-1],
            device_id_type=pl.DeviceIdType.MESH,
        )

    for chunk in range(CHUNKS):
        far_copy(chunk).start()

    first_far = distances_ref[0] == farthest
    distance = jnp.where(first_far, distances_ref[1], distances_ref[0])
    crosses = distance >= blocks // 2
    remaining = jnp.where(crosses, farthest - distance, distance)

    edge = jnp.zeros((channels, LANES), jnp.bfloat16)
    padded_ref[0] = edge
    padded_ref[1] = edge
    padded_ref[pieces + 2] = edge
    far_ref[0] = edge
    far_ref[pieces + 1] = edge
    carried_ref[hops, 0] = edge
    carried_ref[hops, pieces + 1] = edge

    @pl.loop(0, pieces)
    def _(piece):
        padded_ref[piece + 2] = own_ref[piece]

    @pl.loop(0, pieces + 1)
    def _(piece):
        lanes = pl.ds(pl.multiple_of(piece * LANES, LANES), LANES)
        last, now, later = (padded_ref[piece + step].astype(jnp.float32) for step in range(3))
        for coarse in range(COARSE):
            amount = before - FINE * coarse
            if amount >= 0:
                value = shifted(now, later, amount)
            else:
                value = shifted(last, now, LANES + amount)
            left_ref[coarse * channels : (coarse + 1) * channels, lanes] = value.astype(jnp.bfloat16)

    for coarse in range(COARSE):
        row = lax.broadcasted_iota(jnp.int32, table_ref.shape[1:], 0)
        column = lax.broadcasted_iota(jnp.int32, table_ref.shape[1:], 1)
        target = (row & (half - 1)) * LAGS + (row >> (half.bit_length() - 1)) + coarse * FINE
        table_ref[coarse] = jnp.where(column == target, 1.0, 0.0).astype(jnp.bfloat16)

    def multiply(which, load, chunk):
        start = chunk * per_chunk
        count = per_chunk + (1 if chunk == CHUNKS - 1 else 0)

        @pl.loop(0, count)
        def _(step):
            lanes = pl.ds(pl.multiple_of(step * LANES, LANES), LANES)
            now, later = (load(start + step + ahead).astype(jnp.float32) for ahead in range(2))
            for fine in range(FINE):
                value = shifted(now, later, fine).astype(jnp.bfloat16)
                for part in range(2):
                    row = part * width + fine * half
                    right_ref[row : row + half, lanes] = value[part * half : (part + 1) * half]

        product = lax.dot_general(
            left_ref[:, start * LANES : (start + count) * LANES],
            right_ref[:, : count * LANES],
            NT,
            preferred_element_type=jnp.float32,
        )
        for part in range(2):
            addend = product[:, part * width : (part + 1) * width]
            if chunk == 0:
                products_ref[which, part] = addend
            else:
                products_ref[which, part] += addend

    for step in range(CHUNKS + hops):
        for stage in range(hops, -1, -1):
            chunk = step - stage
            if chunk < 0 or chunk >= CHUNKS:
                continue
            inside = pl.ds(1 + chunk * per_chunk, per_chunk)
            plain = pl.ds(chunk * per_chunk, per_chunk)
            if stage == 0:
                far_copy(chunk).wait_recv()
                carried_ref[0, inside] = lax.select(crosses, far_ref[inside], own_ref[plain])
            else:
                hop_copy(stage - 1, chunk).wait_recv()
                chosen = jnp.bitwise_and(jnp.right_shift(remaining, stage - 1), 1) == 1
                carried_ref[stage, inside] = lax.select(
                    chosen, arrived_ref[stage - 1, plain], carried_ref[stage - 1, inside]
                )
            if stage < hops:
                hop_copy(stage, chunk).start()
        if step < CHUNKS:
            multiply(0, lambda index: far_ref[index], step)
            if step == CHUNKS - 1:
                sum_copy(0).start()
        if step >= hops:
            multiply(1, lambda index: carried_ref[hops, index], step - hops)
    sum_copy(1).start()

    def gathered(which):
        total = products_ref[which, seg] + sums_ref[which]
        return jnp.concatenate(
            [total[coarse * channels : (coarse + 1) * channels] for coarse in range(COARSE)], axis=1
        )

    table = table_ref.reshape(COARSE * width, half * LAGS)
    sum_copy(0).wait_recv()
    from_far = arrange(table, [gathered(0)], factor)
    sum_copy(1).wait_recv()
    from_carried = arrange(table, [gathered(1)], factor)
    out_ref[0] = lax.select(first_far, from_far, from_carried)
    out_ref[1] = lax.select(first_far, from_carried, from_far)
    for chunk in range(CHUNKS):
        far_copy(chunk).wait_send()
        for bit in range(hops):
            hop_copy(bit, chunk).wait_send()
    for which in range(2):
        sum_copy(which).wait_send()


def shards(traces, fir_taps, slot_channel, segment_valid, distances):
    _, channels, samples = traces.shape
    pieces = samples // LANES
    half = channels // 2
    width = FINE * half
    vmem = pl.BlockSpec(memory_space=pltpu.VMEM)
    smem = pl.BlockSpec(memory_space=pltpu.SMEM)
    hbm = pl.BlockSpec(memory_space=pltpu.HBM)
    params = pltpu.CompilerParams(vmem_limit_bytes=48 * 2**20)
    whitened = pl.pallas_call(
        whiten_kernel,
        out_shape=jax.ShapeDtypeStruct((pieces, channels, LANES), jnp.bfloat16),
        in_specs=[hbm] * 4,
        out_specs=vmem,
        scratch_shapes=[
            pltpu.SMEM(slot_channel.shape, jnp.int32),
            pltpu.SMEM(segment_valid.shape, jnp.int32),
            pltpu.VMEM(traces.shape, jnp.bfloat16),
            pltpu.VMEM(fir_taps.shape, jnp.bfloat16),
            pltpu.VMEM(((pieces + 2) * channels, LANES), jnp.float32),
            pltpu.VMEM((channels, 3 * LANES), jnp.float32),
            pltpu.VMEM((pieces * channels, LANES), jnp.float32),
            pltpu.SemaphoreType.DMA((4,)),
        ],
        compiler_params=params,
    )(slot_channel, segment_valid, traces, fir_taps)

    blocks = lax.axis_size("sensor")
    hops = (blocks - 1).bit_length() - 1
    factor = 1.0 / math.sqrt(samples * traces.shape[0] * lax.axis_size("seg"))
    depth = (pieces + 1) * LANES
    return pl.pallas_call(
        functools.partial(exchange_kernel, blocks, factor),
        out_shape=jax.ShapeDtypeStruct((2, channels, half * LAGS), jnp.float32),
        in_specs=[smem, vmem],
        out_specs=vmem,
        scratch_shapes=[
            pltpu.VMEM((pieces + 3, channels, LANES), jnp.bfloat16),
            pltpu.VMEM((pieces + 2, channels, LANES), jnp.bfloat16),
            pltpu.VMEM((hops + 1, pieces + 2, channels, LANES), jnp.bfloat16),
            pltpu.VMEM((hops, pieces, channels, LANES), jnp.bfloat16),
            pltpu.VMEM((COARSE * channels, depth), jnp.bfloat16),
            pltpu.VMEM((2 * width, (pieces // CHUNKS + 1) * LANES), jnp.bfloat16),
            pltpu.VMEM((2, 2, COARSE * channels, width), jnp.float32),
            pltpu.VMEM((2, COARSE * channels, width), jnp.float32),
            pltpu.VMEM((COARSE, width, half * LAGS), jnp.bfloat16),
            pltpu.SemaphoreType.DMA((2, CHUNKS)),
            pltpu.SemaphoreType.DMA((2, hops, CHUNKS)),
            pltpu.SemaphoreType.DMA((2, 2)),
        ],
        compiler_params=pltpu.CompilerParams(
            collective_id=0, has_side_effects=True, vmem_limit_bytes=48 * 2**20
        ),
    )(distances, whitened)


def solution(mesh):
    placed = (
        P("seg", ("groups", "sensor"), None),
        P(("groups", "sensor"), None),
        P(("groups", "sensor"), None),
        P("seg", ("groups", "sensor")),
        P(),
    )
    return jax.shard_map(
        shards,
        mesh=mesh,
        in_specs=placed,
        out_specs=P(None, ("groups", "sensor"), "seg"),
        check_vma=False,
    )
```

time: 66 us -> 45.2 us (0.68)
  Pallas kernels: 10.3 us -> 41.3 us
  waiting for transfers between devices: 24.4 us -> 0 us
  between operations: 15.3 us -> 0.03 us
  starting transfers between devices: 10.8 us -> 0 us
  local copies, waits for them, and re-layouts: 4.49 us -> 3.66 us
    pallas_call x3 -> x2, Pallas kernels: 10.3 us -> 41.3 us  [the longest x1 36.3 us: shards(): pl.pallas_call(functools.partial(exchange_kernel, blocks, factor), out_sh...]
    ppermute x3 -> x0, waiting for transfers between devices: 13.5 us -> none  [swapped(): return lax.ppermute(value, 'sensor', pairs)]
    reduce_scatter x1 -> x0, waiting for transfers between devices: 10.9 us -> none  [shards(): summed = lax.psum_scatter(products, 'seg', scatter_dimension=0, tiled=False)]
    ppermute x3 -> x0, starting transfers between devices: 10.8 us -> none  [swapped(): return lax.ppermute(value, 'sensor', pairs)]
    unnamed x12 -> x11, local copies, waits for them, and re-layouts: 3.91 us -> 3.66 us
  transfers between devices with their start and end apart: 4 -> 0, of which waited for: 4 -> 0; matrix products, arithmetic and copies ran while one was open for 1% -> 0% of each run, Pallas kernels for 0% -> 0%
where the time goes in v1:
time: 45.2 us; the launch traced here: 45 us
  Pallas kernels  41.3 us (91%)
  local copies, waits for them, and re-layouts  3.66 us (8%)
    pallas_call x1, Pallas kernels, shards(): pl.pallas_call(functools.partial(exchange_kernel, blocks, factor), out_sh...  36.3 us
    pallas_call x1, Pallas kernels, shards(): pl.pallas_call(whiten_kernel, out_shape=jax.ShapeDtypeStruct((pieces, cha...  5 us
    unnamed x11, local copies, waits for them, and re-layouts  3.66 us

profile of v1, /device:TPU:1, one launch (start us, length us, event | category | flops | bytes accessed | tf_op | source)
XLA Modules:
  0.0 45.0 jit_solution(6190368830959514881)
XLA Ops:
  0.0 0.0 copy-start
  0.0 0.9 %copy-done = bf16[1,32,4096]{2,1,0:T(8,128)(2,1)S(1)} copy-done((bf16[1,32,4096]{2,1,0:T(8,128)(2,1)S(1)}, bf16[1,32,4096]{2,1,0:T(8,128)(2,1)}, u32[]{:S(2)}) %copy-start) | copy-done | bytes 262168
  1.0 0.0 copy-start.1
  1.0 0.7 %copy-done.1 = bf16[32,255]{1,0:T(8,128)(2,1)S(1)} copy-done((bf16[32,255]{1,0:T(8,128)(2,1)S(1)}, bf16[32,255]{1,0:T(8,128)(2,1)}, u32[]{:S(2)}) %copy-start.1) | copy-done | bytes 16344
  1.7 0.0 copy-start.2
  1.7 0.7 %copy-done.2 = s32[1,32]{1,0:T(1,128)S(1)} copy-done((s32[1,32]{1,0:T(1,128)S(1)}, s32[1,32]{1,0:T(1,128)}, u32[]{:S(2)}) %copy-start.2) | copy-done | bytes 152
  2.3 0.0 copy-start.3
  2.3 0.7 %copy-done.3 = s32[1,32]{1,0:T(1,128)S(1)} copy-done((s32[1,32]{1,0:T(1,128)S(1)}, s32[1,32]{1,0:T(1,128)}, u32[]{:S(2)}) %copy-start.3) | copy-done | bytes 152
  3.0 0.0 copy-start.4
  3.0 5.0 %shard_map.55.own_ref = bf16[32,32,128]{2,1,0:T(8,128)(2,1)S(1)} custom-call(s32[1,32]{1,0:T(1,128)S(1)} %copy-done.2, s32[1,32]{1,0:T(1,128)S(1)} %copy-done.3, bf16[1,32,4096]{2,1,0:T(8,128)(2,1)S(1)} %copy-done, bf16[32,255]{1,0:T(8,128)(2,1)S(1)} %copy-done.1), custom_call_target="tpu_custom_call" | custom-call | tf_op jit(solution)/shard_map/pallas_call | solution.py:271
  8.0 0.0 copy-done.4
  8.0 36.3 %shard_map.56 = f32[2,32,768]{2,1,0:T(8,128)S(1)} custom-call(s32[2]{0:T(128)S(1)} %copy-done.4, bf16[32,32,128]{2,1,0:T(8,128)(2,1)S(1)} %shard_map.55.own_ref), custom_call_target="tpu_custom_call" | custom-call | tf_op jit(solution)/shard_map/pallas_call | solution.py:293
  44.3 0.7 %copy.7 = f32[2,32,768]{2,1,0:T(8,128)} copy(f32[2,32,768]{2,1,0:T(8,128)S(1)} %shard_map.56) | data formatting | bytes 393216
Async XLA Ops:
  0.0 0.9 %copy-start = (bf16[1,32,4096]{2,1,0:T(8,128)(2,1)S(1)}, bf16[1,32,4096]{2,1,0:T(8,128)(2,1)}, u32[]{:S(2)}) copy-start(bf16[1,32,4096]{2,1,0:T(8,128)(2,1)} %traces_hbm.1) | copy-start | bytes 786436
  1.0 0.7 %copy-start.1 = (bf16[32,255]{1,0:T(8,128)(2,1)S(1)}, bf16[32,255]{1,0:T(8,128)(2,1)}, u32[]{:S(2)}) copy-start(bf16[32,255]{1,0:T(8,128)(2,1)} %taps_hbm.1) | copy-start | bytes 48964
  1.7 0.7 %copy-start.2 = (s32[1,32]{1,0:T(1,128)S(1)}, s32[1,32]{1,0:T(1,128)}, u32[]{:S(2)}) copy-start(s32[1,32]{1,0:T(1,128)} %slot_hbm.1) | copy-start | bytes 388
  2.3 0.7 %copy-start.3 = (s32[1,32]{1,0:T(1,128)S(1)}, s32[1,32]{1,0:T(1,128)}, u32[]{:S(2)}) copy-start(s32[1,32]{1,0:T(1,128)} %valid_hbm.1) | copy-start | bytes 388
  3.0 5.0 %copy-start.4 = (s32[2]{0:T(128)S(1)}, s32[2]{0:T(128)}, u32[]{:S(2)}) copy-start(s32[2]{0:T(128)} %distances_ref.1) | copy-start | bytes 28

commit v2 on v1

--- a/solution.py
+++ b/solution.py
@@ -13,6 +13,7 @@
 COARSE = LAGS // FINE
 LANES = 128
 CHUNKS = 4
+SLACK = 2
 EPSILON = 1e-06
 NT = (((1,), (1,)), ((), ()))
 
@@ -146,7 +147,7 @@
             device_id_type=pl.DeviceIdType.MESH,
         )
 
-    for chunk in range(CHUNKS):
+    for chunk in range(min(2, CHUNKS)):
         far_copy(chunk).start()
 
     first_far = distances_ref[0] == farthest
@@ -167,7 +168,7 @@
     def _(piece):
         padded_ref[piece + 2] = own_ref[piece]
 
-    @pl.loop(0, pieces + 1)
+    @pl.loop(0, pieces + 1, unroll=3)
     def _(piece):
         lanes = pl.ds(pl.multiple_of(piece * LANES, LANES), LANES)
         last, now, later = (padded_ref[piece + step].astype(jnp.float32) for step in range(3))
@@ -189,7 +190,7 @@
         start = chunk * per_chunk
         count = per_chunk + (1 if chunk == CHUNKS - 1 else 0)
 
-        @pl.loop(0, count)
+        @pl.loop(0, count, unroll=count)
         def _(step):
             lanes = pl.ds(pl.multiple_of(step * LANES, LANES), LANES)
             now, later = (load(start + step + ahead).astype(jnp.float32) for ahead in range(2))
@@ -212,9 +213,9 @@
             else:
                 products_ref[which, part] += addend
 
-    for step in range(CHUNKS + hops):
+    for step in range(CHUNKS + SLACK * hops):
         for stage in range(hops, -1, -1):
-            chunk = step - stage
+            chunk = step - SLACK * stage
             if chunk < 0 or chunk >= CHUNKS:
                 continue
             inside = pl.ds(1 + chunk * per_chunk, per_chunk)
@@ -230,12 +231,14 @@
                 )
             if stage < hops:
                 hop_copy(stage, chunk).start()
+            if stage == 0 and chunk + 2 < CHUNKS:
+                far_copy(chunk + 2).start()
         if step < CHUNKS:
             multiply(0, lambda index: far_ref[index], step)
             if step == CHUNKS - 1:
                 sum_copy(0).start()
-        if step >= hops:
-            multiply(1, lambda index: carried_ref[hops, index], step - hops)
+        if step >= SLACK * hops:
+            multiply(1, lambda index: carried_ref[hops, index], step - SLACK * hops)
     sum_copy(1).start()
 
     def gathered(which):
@@ -267,7 +270,7 @@
     vmem = pl.BlockSpec(memory_space=pltpu.VMEM)
     smem = pl.BlockSpec(memory_space=pltpu.SMEM)
     hbm = pl.BlockSpec(memory_space=pltpu.HBM)
-    params = pltpu.CompilerParams(vmem_limit_bytes=48 * 2**20)
+    params = pltpu.CompilerParams(vmem_limit_bytes=64 * 2**20 - 2**17)
     whitened = pl.pallas_call(
         whiten_kernel,
         out_shape=jax.ShapeDtypeStruct((pieces, channels, LANES), jnp.bfloat16),

time: 45.2 us -> 35.8 us (0.79)
  Pallas kernels: 41.3 us -> 34 us
  local copies, waits for them, and re-layouts: 3.66 us -> 1.63 us
    pallas_call x1, Pallas kernels: 36.3 us -> 27.9 us  [shards(): pl.pallas_call(functools.partial(exchange_kernel, blocks, factor), out_sh...]
    unnamed x11 -> x5, local copies, waits for them, and re-layouts: 3.66 us -> 1.63 us
    pallas_call x1, Pallas kernels: 5 us -> 6.09 us  [shards(): pl.pallas_call(whiten_kernel, out_shape=jax.ShapeDtypeStruct((pieces, cha...]
where the time goes in v2:
time: 35.8 us; the launch traced here: 35.7 us
  Pallas kernels  34 us (95%)
  local copies, waits for them, and re-layouts  1.63 us (5%)
    pallas_call x1, Pallas kernels, shards(): pl.pallas_call(functools.partial(exchange_kernel, blocks, factor), out_sh...  27.9 us
    pallas_call x1, Pallas kernels, shards(): pl.pallas_call(whiten_kernel, out_shape=jax.ShapeDtypeStruct((pieces, cha...  6.09 us
    unnamed x5, local copies, waits for them, and re-layouts  1.63 us

profile of v2, /device:TPU:1, one launch (start us, length us, event | category | flops | bytes accessed | tf_op | source)
XLA Modules:
  0.0 35.7 jit_solution(12586169779718553651)
XLA Ops:
  0.0 0.0 copy-start.1
  0.0 6.1 %shard_map.55.own_ref = bf16[32,32,128]{2,1,0:T(8,128)(2,1)} custom-call(s32[1,32]{1,0:T(1,128)} %slot_hbm.1, s32[1,32]{1,0:T(1,128)} %valid_hbm.1, bf16[1,32,4096]{2,1,0:T(8,128)(2,1)} %traces_hbm.1, bf16[32,255]{1,0:T(8,128)(2,1)} %taps_hbm.1), custom_call_target="tpu_custom_call" | custom-call | tf_op jit(solution)/shard_map/pallas_call | solution.py:274
  6.1 0.0 copy-done.1
  6.1 0.0 copy-start
  6.1 0.9 %copy-done = bf16[32,32,128]{2,1,0:T(8,128)(2,1)S(1)} copy-done((bf16[32,32,128]{2,1,0:T(8,128)(2,1)S(1)}, bf16[32,32,128]{2,1,0:T(8,128)(2,1)}, u32[]{:S(2)}) %copy-start) | copy-done | bytes 262168
  7.1 27.9 %shard_map.56 = f32[2,32,768]{2,1,0:T(8,128)S(1)} custom-call(s32[2]{0:T(128)S(1)} %copy-done.1, bf16[32,32,128]{2,1,0:T(8,128)(2,1)S(1)} %copy-done), custom_call_target="tpu_custom_call" | custom-call | tf_op jit(solution)/shard_map/pallas_call | solution.py:296
  35.0 0.7 %copy.7 = f32[2,32,768]{2,1,0:T(8,128)} copy(f32[2,32,768]{2,1,0:T(8,128)S(1)} %shard_map.56) | data formatting | bytes 393216
Async XLA Ops:
  0.0 6.1 %copy-start.1 = (s32[2]{0:T(128)S(1)}, s32[2]{0:T(128)}, u32[]{:S(2)}) copy-start(s32[2]{0:T(128)} %distances_ref.1) | copy-start | bytes 28
  6.1 1.0 %copy-start = (bf16[32,32,128]{2,1,0:T(8,128)(2,1)S(1)}, bf16[32,32,128]{2,1,0:T(8,128)(2,1)}, u32[]{:S(2)}) copy-start(bf16[32,32,128]{2,1,0:T(8,128)(2,1)} %shard_map.55.own_ref) | copy-start | bytes 786436

commit v3 on v2

--- a/solution.py
+++ b/solution.py
@@ -13,7 +13,7 @@
 COARSE = LAGS // FINE
 LANES = 128
 CHUNKS = 4
-SLACK = 2
+SLACK = 3
 EPSILON = 1e-06
 NT = (((1,), (1,)), ((), ()))
 
@@ -127,13 +127,17 @@
             device_id_type=pl.DeviceIdType.MESH,
         )
 
+    def hop_partner(bit):
+        up, down = others[1 + bit]["sensor"], others[hops - bit]["sensor"]
+        return {"sensor": up + seg * (down - up)}
+
     def hop_copy(bit, chunk):
         return pltpu.make_async_remote_copy(
             src_ref=carried_ref.at[bit, pl.ds(1 + chunk * per_chunk, per_chunk)],
             dst_ref=arrived_ref.at[bit, pl.ds(chunk * per_chunk, per_chunk)],
             send_sem=hop_sems.at[0, bit, chunk],
             recv_sem=hop_sems.at[1, bit, chunk],
-            device_id=others[1 + bit],
+            device_id=hop_partner(bit),
             device_id_type=pl.DeviceIdType.MESH,
         )
 
@@ -225,7 +229,7 @@
                 carried_ref[0, inside] = lax.select(crosses, far_ref[inside], own_ref[plain])
             else:
                 hop_copy(stage - 1, chunk).wait_recv()
-                chosen = jnp.bitwise_and(jnp.right_shift(remaining, stage - 1), 1) == 1
+                chosen = jnp.bitwise_and(jnp.right_shift(remaining, stage - 1 + seg * (hops + 1 - 2 * stage)), 1) == 1
                 carried_ref[stage, inside] = lax.select(
                     chosen, arrived_ref[stage - 1, plain], carried_ref[stage - 1, inside]
                 )

time: 35.8 us -> 35.3 us (0.986)
  Pallas kernels: 34 us -> 33.5 us
    pallas_call x1, Pallas kernels: 27.9 us -> 27.4 us  [shards(): pl.pallas_call(functools.partial(exchange_kernel, blocks, factor), out_sh...]
where the time goes in v3:
time: 35.3 us; the launch traced here: 35.2 us
  Pallas kernels  33.5 us (95%)
  local copies, waits for them, and re-layouts  1.63 us (5%)
    pallas_call x1, Pallas kernels, shards(): pl.pallas_call(functools.partial(exchange_kernel, blocks, factor), out_sh...  27.4 us
    pallas_call x1, Pallas kernels, shards(): pl.pallas_call(whiten_kernel, out_shape=jax.ShapeDtypeStruct((pieces, cha...  6.08 us
    unnamed x5, local copies, waits for them, and re-layouts  1.63 us

profile of v3, /device:TPU:1, one launch (start us, length us, event | category | flops | bytes accessed | tf_op | source)
XLA Modules:
  0.0 35.2 jit_solution(1753980386868348736)
XLA Ops:
  0.0 0.0 copy-start.1
  0.0 6.1 %shard_map.55.own_ref = bf16[32,32,128]{2,1,0:T(8,128)(2,1)} custom-call(s32[1,32]{1,0:T(1,128)} %slot_hbm.1, s32[1,32]{1,0:T(1,128)} %valid_hbm.1, bf16[1,32,4096]{2,1,0:T(8,128)(2,1)} %traces_hbm.1, bf16[32,255]{1,0:T(8,128)(2,1)} %taps_hbm.1), custom_call_target="tpu_custom_call" | custom-call | tf_op jit(solution)/shard_map/pallas_call | solution.py:278
  6.1 0.0 copy-done.1
  6.1 0.0 copy-start
  6.1 0.9 %copy-done = bf16[32,32,128]{2,1,0:T(8,128)(2,1)S(1)} copy-done((bf16[32,32,128]{2,1,0:T(8,128)(2,1)S(1)}, bf16[32,32,128]{2,1,0:T(8,128)(2,1)}, u32[]{:S(2)}) %copy-start) | copy-done | bytes 262168
  7.1 27.4 %shard_map.56 = f32[2,32,768]{2,1,0:T(8,128)S(1)} custom-call(s32[2]{0:T(128)S(1)} %copy-done.1, bf16[32,32,128]{2,1,0:T(8,128)(2,1)S(1)} %copy-done), custom_call_target="tpu_custom_call" | custom-call | tf_op jit(solution)/shard_map/pallas_call | solution.py:300
  34.5 0.7 %copy.7 = f32[2,32,768]{2,1,0:T(8,128)} copy(f32[2,32,768]{2,1,0:T(8,128)S(1)} %shard_map.56) | data formatting | bytes 393216
Async XLA Ops:
  0.0 6.1 %copy-start.1 = (s32[2]{0:T(128)S(1)}, s32[2]{0:T(128)}, u32[]{:S(2)}) copy-start(s32[2]{0:T(128)} %distances_ref.1) | copy-start | bytes 28
  6.1 1.0 %copy-start = (bf16[32,32,128]{2,1,0:T(8,128)(2,1)S(1)}, bf16[32,32,128]{2,1,0:T(8,128)(2,1)}, u32[]{:S(2)}) copy-start(bf16[32,32,128]{2,1,0:T(8,128)(2,1)} %shard_map.55.own_ref) | copy-start | bytes 786436

commit v4 on v3

--- a/solution.py
+++ b/solution.py
@@ -46,7 +46,7 @@
     taps_f32[...] = jnp.zeros_like(taps_f32)
     taps_f32[:, 0:tap_count] = taps_ref[...].astype(jnp.float32)
 
-    @pl.loop(0, channels, unroll=4)
+    @pl.loop(0, channels, unroll=8)
     def _(slot):
         channel = slot_ref[0, slot]
         usable = valid_ref[0, channel].astype(jnp.float32)

time: 35.3 us -> 34.2 us (0.969)
  Pallas kernels: 33.5 us -> 32.4 us
    pallas_call x1, Pallas kernels: 6.08 us -> 4.96 us  [shards(): pl.pallas_call(whiten_kernel, out_shape=jax.ShapeDtypeStruct((pieces, cha...]
where the time goes in v4:
time: 34.2 us; the launch traced here: 34.1 us
  Pallas kernels  32.4 us (95%)
  local copies, waits for them, and re-layouts  1.63 us (5%)
    pallas_call x1, Pallas kernels, shards(): pl.pallas_call(functools.partial(exchange_kernel, blocks, factor), out_sh...  27.4 us
    pallas_call x1, Pallas kernels, shards(): pl.pallas_call(whiten_kernel, out_shape=jax.ShapeDtypeStruct((pieces, cha...  4.96 us
    unnamed x5, local copies, waits for them, and re-layouts  1.63 us

profile of v4, /device:TPU:1, one launch (start us, length us, event | category | flops | bytes accessed | tf_op | source)
XLA Modules:
  0.0 34.1 jit_solution(13956504600046145714)
XLA Ops:
  0.0 0.0 copy-start.1
  0.0 5.0 %shard_map.55.own_ref = bf16[32,32,128]{2,1,0:T(8,128)(2,1)} custom-call(s32[1,32]{1,0:T(1,128)} %slot_hbm.1, s32[1,32]{1,0:T(1,128)} %valid_hbm.1, bf16[1,32,4096]{2,1,0:T(8,128)(2,1)} %traces_hbm.1, bf16[32,255]{1,0:T(8,128)(2,1)} %taps_hbm.1), custom_call_target="tpu_custom_call" | custom-call | tf_op jit(solution)/shard_map/pallas_call | solution.py:278
  5.0 0.0 copy-done.1
  5.0 0.0 copy-start
  5.0 0.9 %copy-done = bf16[32,32,128]{2,1,0:T(8,128)(2,1)S(1)} copy-done((bf16[32,32,128]{2,1,0:T(8,128)(2,1)S(1)}, bf16[32,32,128]{2,1,0:T(8,128)(2,1)}, u32[]{:S(2)}) %copy-start) | copy-done | bytes 262168
  5.9 27.4 %shard_map.56 = f32[2,32,768]{2,1,0:T(8,128)S(1)} custom-call(s32[2]{0:T(128)S(1)} %copy-done.1, bf16[32,32,128]{2,1,0:T(8,128)(2,1)S(1)} %copy-done), custom_call_target="tpu_custom_call" | custom-call | tf_op jit(solution)/shard_map/pallas_call | solution.py:300
  33.4 0.7 %copy.7 = f32[2,32,768]{2,1,0:T(8,128)} copy(f32[2,32,768]{2,1,0:T(8,128)S(1)} %shard_map.56) | data formatting | bytes 393216
Async XLA Ops:
  0.0 5.0 %copy-start.1 = (s32[2]{0:T(128)S(1)}, s32[2]{0:T(128)}, u32[]{:S(2)}) copy-start(s32[2]{0:T(128)} %distances_ref.1) | copy-start | bytes 28
  5.0 1.0 %copy-start = (bf16[32,32,128]{2,1,0:T(8,128)(2,1)S(1)}, bf16[32,32,128]{2,1,0:T(8,128)(2,1)}, u32[]{:S(2)}) copy-start(bf16[32,32,128]{2,1,0:T(8,128)(2,1)} %shard_map.55.own_ref) | copy-start | bytes 786436
